TPU v7x, 32 devices: a whole 2x2x4 slice. The times are simulated.
32 devices in a mesh: lat: 8 (over z, y), lon: 2 (over x), head: 2 (over core).
Axes of the slice: x: 2, y: 2, z: 4, core: 2. Of those that a mesh axis runs over, the one named last changes fastest.
Arguments:
- queries: bfloat16 [8, 2, 512, 1024], P('lat', 'lon', None, 'head'), may hold values from -250 to 250, as said below
- key_value: bfloat16 [8, 2, 512, 128], P('lat', 'lon'), may hold values from -5 to 5
- dout: bfloat16 [8, 2, 512, 1024], P('lat', 'lon', None, 'head'), may hold values from -6 to 6
Outputs:
- dquery: bfloat16 [8, 2, 512, 1024], P('lat', 'lon', None, 'head')
- dkey_value: float32 [8, 2, 512, 128], P('lat', 'lon', 'head')
Inputs may be any that keep to these rules, and one draw needn't show every extreme that they name: `queries`: queries and keys have entries of order one, except that some query rows may be large multiples of nearby keys.
All inputs are finite; a program needn't handle non-finite values.
Results may differ from a plain program's by a relative error of at most 0.005.
Values may be sent and summed in bfloat16 or wider, within the bound.
A program may use at most 64 MiB of HBM per device.

v0:
```python
import jax
import jax.numpy as jnp
from jax import lax
from jax.sharding import PartitionSpec as P

HEAD_DIM = 64


def passed_along(array, axis, by):
    peers = lax.axis_size(axis)
    return lax.ppermute(array, axis, [(i, (i + by) % peers) for i in range(peers)])


def gather_near(tile):
    pieces = []
    for step in (-2, 2):
        pieces.append(passed_along(tile, "lat", step))
    for step in (-2, 2):
        pieces.append(passed_along(tile, "lon", step))
    return jnp.stack(pieces)


def send_back(parts):
    total = parts[0]
    offsets = (-2, 2)
    for index in range(2):
        total = total + passed_along(
            parts[1 + index].astype(jnp.bfloat16), "lat", -offsets[index]
        ).astype(jnp.float32)
    for index in range(2):
        total = total + passed_along(
            parts[3 + index].astype(jnp.bfloat16), "lon", -offsets[index]
        ).astype(jnp.float32)
    return total


def local(queries, key_value, dout):
    tile = key_value[0, 0]
    tokens = tile.shape[0]
    local_heads = queries.shape[3] // HEAD_DIM
    scale = 1.0 / HEAD_DIM**0.5
    near = gather_near(tile)
    key_set = jnp.concatenate([tile[None], near], axis=0).reshape(5 * tokens, 2 * HEAD_DIM)
    keys = key_set[:, :HEAD_DIM]
    values = key_set[:, HEAD_DIM:]
    q_heads = queries[0, 0].reshape(tokens, local_heads, HEAD_DIM).transpose(1, 0, 2)
    d_heads = dout[0, 0].reshape(tokens, local_heads, HEAD_DIM).transpose(1, 0, 2)

    def one_head(carry, operands):
        q_one, d_one = operands
        scores = jnp.dot(q_one, keys.T, preferred_element_type=jnp.float32) * scale
        top = jnp.max(scores, axis=-1, keepdims=True)
        expo = jnp.exp(scores - top)
        probs = expo / jnp.sum(expo, axis=-1, keepdims=True)
        probs_low = probs.astype(jnp.bfloat16)
        dprobs = jnp.dot(d_one, values.T, preferred_element_type=jnp.float32)
        delta = jnp.sum(probs * dprobs, axis=-1, keepdims=True)
        dscore = (probs * (dprobs - delta) * scale).astype(jnp.bfloat16)
        dq_one = jnp.dot(dscore, keys, preferred_element_type=jnp.float32).astype(jnp.bfloat16)
        dkeys = jnp.dot(dscore.T, q_one, preferred_element_type=jnp.float32)
        dvalues = jnp.dot(probs_low.T, d_one, preferred_element_type=jnp.float32)
        return (carry + jnp.concatenate([dkeys, dvalues], axis=1), dq_one)

    start = jnp.zeros((5 * tokens, 2 * HEAD_DIM), jnp.float32)
    grads, dq_heads = lax.scan(one_head, start, (q_heads, d_heads))
    dquery = dq_heads.transpose(1, 0, 2).reshape(tokens, local_heads * HEAD_DIM)[None, None]
    parts = grads.reshape(5, tokens, 2 * HEAD_DIM)
    total = lax.psum_scatter(send_back(parts), "head", scatter_dimension=0, tiled=True)
    return (dquery, total[None, None])


def solution(mesh):
    placed = (
        P("lat", "lon", None, "head"),
        P("lat", "lon", None, None),
        P("lat", "lon", None, "head"),
    )
    return jax.shard_map(
        local,
        mesh=mesh,
        in_specs=placed,
        out_specs=(P("lat", "lon", None, "head"), P("lat", "lon", "head", None)),
        check_vma=False,
    )
```

profile of v0, /device:TPU:0, one launch (start us, length us, event | category | flops | bytes accessed | tf_op | source)
XLA Modules:
  0.0 178.8 jit_solution(8648894284266007319)
XLA Ops:
  7.2 5.1 %collective-permute-start = (bf16[512,128]{1,0:T(8,128)(2,1)}, bf16[512,128]{1,0:T(8,128)(2,1)S(1)}, u32[]{:S(2)}, u32[]{:S(2)}) collective-permute-start(bf16[512,128]{1,0:T(8,128)(2,1)} %bitcast.70), channel_id=1, source_target_pairs={{0,24},{4,28},{8,0},{12,4},{16,8},{20,12},{24,16},{28,20},{1,25},{... | collective-permute-start | bytes 393224 | tf_op jit(solution)/shard_map/ppermute | solution.py:11
  20.5 132.4 %while.13 = (s32[]{:T(128)}, f32[2560,128]{0,1:T(8,128)}, bf16[8,512,64]{1,2,0:T(8,128)(2,1)}, bf16[8,512,64]{1,2,0:T(8,128)(2,1)}, bf16[2560,64]{1,0:T(8,128)(2...) while((s32[]{:T(128)}, f32[2560,128]{0,1:T(8,128)}, ...), condition=%wide.region_4.5_spmd.clone, body=%wide.region_0.4_spmd.clone.sunk | while | flops 862157312 | bytes 51470948 | solution.py:65
  23.1 2.7 %multiply_reduce_fusion.2 = (f32[512]{0:T(512)S(1)}, f32[512,2560]{1,0:T(8,128)S(1)}) fusion(f32[512]{0:T(512)S(1)} %fusion.54, f32[512,2560]{1,0:T(8,128)S(1)} %get-tuple-element.146, f32[512]{0:T(512)S(1)} %get-tuple-element.147, bf16[2560,64]{1,0:T(8,128)(2,1)} %get-tuple-element.174, bf16[8,512,64]{1,2,0:T(8,128)(2,1)} %get-tuple-element.173, ...), kind=kOutput, calls=%fused_computation.1.clone.1 | convolution fusion | flops 173014528 | bytes 11213312 | tf_op jit(solution)/shard_map/while/body/eval_jaxpr/dot_general | solution.py:56
  27.6 2.3 %fusion.56 = f32[2560,64]{0,1:T(8,128)} fusion(bf16[512,2560]{1,0:T(8,128)(2,1)S(1)} %multiply_convert_fusion.2, bf16[8,512,64]{1,2,0:T(8,128)(2,1)} %get-tuple-element.171, s32[]{:T(128)} %get-tuple-element.159), kind=kOutput, calls=%fused_computation.15.clone.1 | convolution fusion | flops 167772160 | bytes 3342848 | tf_op jit(solution)/shard_map/while/body/eval_jaxpr/dot_general | solution.py:60
  29.8 2.8 %fusion.55 = f32[2560,64]{0,1:T(8,128)} fusion(bf16[8,512,64]{1,2,0:T(8,128)(2,1)} %get-tuple-element.173, s32[]{:T(128)} %get-tuple-element.159, f32[512,2560]{1,0:T(8,128)S(1)} %get-tuple-element.146, f32[512]{0:T(512)S(1)} %fusion.54, f32[512]{0:T(512)S(1)} %get-tuple-element.147), kind=kOutput, calls=%fused_computation.6.clone.1 | convolution fusion | flops 171704320 | bytes 5968384 | tf_op jit(solution)/shard_map/while/body/eval_jaxpr/dot_general | solution.py:61
  32.6 2.5 %maximum_add_fusion.2 = f32[2560,128]{0,1:T(8,128)} fusion(f32[2560,64]{0,1:T(8,128)} %fusion.55, f32[2560,64]{0,1:T(8,128)} %fusion.56, f32[2560,128]{0,1:T(8,128)} %get-tuple-element.160, pred[]{:T(512)S(6)} %compare.3), kind=kLoop, calls=%fused_computation.8.clone.1 | loop fusion | flops 983040 | bytes 3932161 | tf_op jit(solution)/shard_map/while/body/eval_jaxpr/add | solution.py:62
  39.3 2.7 %multiply_reduce_fusion.2 = (f32[512]{0:T(512)S(1)}, f32[512,2560]{1,0:T(8,128)S(1)}) fusion(f32[512]{0:T(512)S(1)} %fusion.54, f32[512,2560]{1,0:T(8,128)S(1)} %get-tuple-element.146, f32[512]{0:T(512)S(1)} %get-tuple-element.147, bf16[2560,64]{1,0:T(8,128)(2,1)} %get-tuple-element.174, bf16[8,512,64]{1,2,0:T(8,128)(2,1)} %get-tuple-element.173, ...), kind=kOutput, calls=%fused_computation.1.clone.1 | convolution fusion | flops 173014528 | bytes 11213312 | tf_op jit(solution)/shard_map/while/body/eval_jaxpr/dot_general | solution.py:56
  43.7 2.3 %fusion.56 = f32[2560,64]{0,1:T(8,128)} fusion(bf16[512,2560]{1,0:T(8,128)(2,1)S(1)} %multiply_convert_fusion.2, bf16[8,512,64]{1,2,0:T(8,128)(2,1)} %get-tuple-element.171, s32[]{:T(128)} %get-tuple-element.159), kind=kOutput, calls=%fused_computation.15.clone.1 | convolution fusion | flops 167772160 | bytes 3342848 | tf_op jit(solution)/shard_map/while/body/eval_jaxpr/dot_general | solution.py:60
  46.0 2.8 %fusion.55 = f32[2560,64]{0,1:T(8,128)} fusion(bf16[8,512,64]{1,2,0:T(8,128)(2,1)} %get-tuple-element.173, s32[]{:T(128)} %get-tuple-element.159, f32[512,2560]{1,0:T(8,128)S(1)} %get-tuple-element.146, f32[512]{0:T(512)S(1)} %fusion.54, f32[512]{0:T(512)S(1)} %get-tuple-element.147), kind=kOutput, calls=%fused_computation.6.clone.1 | convolution fusion | flops 171704320 | bytes 5968384 | tf_op jit(solution)/shard_map/while/body/eval_jaxpr/dot_general | solution.py:61
  48.8 2.9 %maximum_add_fusion.2 = f32[2560,128]{0,1:T(8,128)} fusion(f32[2560,64]{0,1:T(8,128)} %fusion.55, f32[2560,64]{0,1:T(8,128)} %fusion.56, f32[2560,128]{0,1:T(8,128)} %get-tuple-element.160, pred[]{:T(512)S(6)} %compare.3), kind=kLoop, calls=%fused_computation.8.clone.1 | loop fusion | flops 983040 | bytes 3932161 | tf_op jit(solution)/shard_map/while/body/eval_jaxpr/add | solution.py:62
  55.9 2.7 %multiply_reduce_fusion.2 = (f32[512]{0:T(512)S(1)}, f32[512,2560]{1,0:T(8,128)S(1)}) fusion(f32[512]{0:T(512)S(1)} %fusion.54, f32[512,2560]{1,0:T(8,128)S(1)} %get-tuple-element.146, f32[512]{0:T(512)S(1)} %get-tuple-element.147, bf16[2560,64]{1,0:T(8,128)(2,1)} %get-tuple-element.174, bf16[8,512,64]{1,2,0:T(8,128)(2,1)} %get-tuple-element.173, ...), kind=kOutput, calls=%fused_computation.1.clone.1 | convolution fusion | flops 173014528 | bytes 11213312 | tf_op jit(solution)/shard_map/while/body/eval_jaxpr/dot_general | solution.py:56
  60.4 2.3 %fusion.56 = f32[2560,64]{0,1:T(8,128)} fusion(bf16[512,2560]{1,0:T(8,128)(2,1)S(1)} %multiply_convert_fusion.2, bf16[8,512,64]{1,2,0:T(8,128)(2,1)} %get-tuple-element.171, s32[]{:T(128)} %get-tuple-element.159), kind=kOutput, calls=%fused_computation.15.clone.1 | convolution fusion | flops 167772160 | bytes 3342848 | tf_op jit(solution)/shard_map/while/body/eval_jaxpr/dot_general | solution.py:60
  62.6 2.8 %fusion.55 = f32[2560,64]{0,1:T(8,128)} fusion(bf16[8,512,64]{1,2,0:T(8,128)(2,1)} %get-tuple-element.173, s32[]{:T(128)} %get-tuple-element.159, f32[512,2560]{1,0:T(8,128)S(1)} %get-tuple-element.146, f32[512]{0:T(512)S(1)} %fusion.54, f32[512]{0:T(512)S(1)} %get-tuple-element.147), kind=kOutput, calls=%fused_computation.6.clone.1 | convolution fusion | flops 171704320 | bytes 5968384 | tf_op jit(solution)/shard_map/while/body/eval_jaxpr/dot_general | solution.py:61
  65.4 2.9 %maximum_add_fusion.2 = f32[2560,128]{0,1:T(8,128)} fusion(f32[2560,64]{0,1:T(8,128)} %fusion.55, f32[2560,64]{0,1:T(8,128)} %fusion.56, f32[2560,128]{0,1:T(8,128)} %get-tuple-element.160, pred[]{:T(512)S(6)} %compare.3), kind=kLoop, calls=%fused_computation.8.clone.1 | loop fusion | flops 983040 | bytes 3932161 | tf_op jit(solution)/shard_map/while/body/eval_jaxpr/add | solution.py:62
  72.5 2.7 %multiply_reduce_fusion.2 = (f32[512]{0:T(512)S(1)}, f32[512,2560]{1,0:T(8,128)S(1)}) fusion(f32[512]{0:T(512)S(1)} %fusion.54, f32[512,2560]{1,0:T(8,128)S(1)} %get-tuple-element.146, f32[512]{0:T(512)S(1)} %get-tuple-element.147, bf16[2560,64]{1,0:T(8,128)(2,1)} %get-tuple-element.174, bf16[8,512,64]{1,2,0:T(8,128)(2,1)} %get-tuple-element.173, ...), kind=kOutput, calls=%fused_computation.1.clone.1 | convolution fusion | flops 173014528 | bytes 11213312 | tf_op jit(solution)/shard_map/while/body/eval_jaxpr/dot_general | solution.py:56
  79.2 2.8 %fusion.55 = f32[2560,64]{0,1:T(8,128)} fusion(bf16[8,512,64]{1,2,0:T(8,128)(2,1)} %get-tuple-element.173, s32[]{:T(128)} %get-tuple-element.159, f32[512,2560]{1,0:T(8,128)S(1)} %get-tuple-element.146, f32[512]{0:T(512)S(1)} %fusion.54, f32[512]{0:T(512)S(1)} %get-tuple-element.147), kind=kOutput, calls=%fused_computation.6.clone.1 | convolution fusion | flops 171704320 | bytes 5968384 | tf_op jit(solution)/shard_map/while/body/eval_jaxpr/dot_general | solution.py:61
  82.0 2.9 %maximum_add_fusion.2 = f32[2560,128]{0,1:T(8,128)} fusion(f32[2560,64]{0,1:T(8,128)} %fusion.55, f32[2560,64]{0,1:T(8,128)} %fusion.56, f32[2560,128]{0,1:T(8,128)} %get-tuple-element.160, pred[]{:T(512)S(6)} %compare.3), kind=kLoop, calls=%fused_computation.8.clone.1 | loop fusion | flops 983040 | bytes 3932161 | tf_op jit(solution)/shard_map/while/body/eval_jaxpr/add | solution.py:62
  89.1 2.7 %multiply_reduce_fusion.2 = (f32[512]{0:T(512)S(1)}, f32[512,2560]{1,0:T(8,128)S(1)}) fusion(f32[512]{0:T(512)S(1)} %fusion.54, f32[512,2560]{1,0:T(8,128)S(1)} %get-tuple-element.146, f32[512]{0:T(512)S(1)} %get-tuple-element.147, bf16[2560,64]{1,0:T(8,128)(2,1)} %get-tuple-element.174, bf16[8,512,64]{1,2,0:T(8,128)(2,1)} %get-tuple-element.173, ...), kind=kOutput, calls=%fused_computation.1.clone.1 | convolution fusion | flops 173014528 | bytes 11213312 | tf_op jit(solution)/shard_map/while/body/eval_jaxpr/dot_general | solution.py:56
  95.8 2.8 %fusion.55 = f32[2560,64]{0,1:T(8,128)} fusion(bf16[8,512,64]{1,2,0:T(8,128)(2,1)} %get-tuple-element.173, s32[]{:T(128)} %get-tuple-element.159, f32[512,2560]{1,0:T(8,128)S(1)} %get-tuple-element.146, f32[512]{0:T(512)S(1)} %fusion.54, f32[512]{0:T(512)S(1)} %get-tuple-element.147), kind=kOutput, calls=%fused_computation.6.clone.1 | convolution fusion | flops 171704320 | bytes 5968384 | tf_op jit(solution)/shard_map/while/body/eval_jaxpr/dot_general | solution.py:61
  98.6 2.9 %maximum_add_fusion.2 = f32[2560,128]{0,1:T(8,128)} fusion(f32[2560,64]{0,1:T(8,128)} %fusion.55, f32[2560,64]{0,1:T(8,128)} %fusion.56, f32[2560,128]{0,1:T(8,128)} %get-tuple-element.160, pred[]{:T(512)S(6)} %compare.3), kind=kLoop, calls=%fused_computation.8.clone.1 | loop fusion | flops 983040 | bytes 3932161 | tf_op jit(solution)/shard_map/while/body/eval_jaxpr/add | solution.py:62
  105.7 2.7 %multiply_reduce_fusion.2 = (f32[512]{0:T(512)S(1)}, f32[512,2560]{1,0:T(8,128)S(1)}) fusion(f32[512]{0:T(512)S(1)} %fusion.54, f32[512,2560]{1,0:T(8,128)S(1)} %get-tuple-element.146, f32[512]{0:T(512)S(1)} %get-tuple-element.147, bf16[2560,64]{1,0:T(8,128)(2,1)} %get-tuple-element.174, bf16[8,512,64]{1,2,0:T(8,128)(2,1)} %get-tuple-element.173, ...), kind=kOutput, calls=%fused_computation.1.clone.1 | convolution fusion | flops 173014528 | bytes 11213312 | tf_op jit(solution)/shard_map/while/body/eval_jaxpr/dot_general | solution.py:56
  112.4 2.8 %fusion.55 = f32[2560,64]{0,1:T(8,128)} fusion(bf16[8,512,64]{1,2,0:T(8,128)(2,1)} %get-tuple-element.173, s32[]{:T(128)} %get-tuple-element.159, f32[512,2560]{1,0:T(8,128)S(1)} %get-tuple-element.146, f32[512]{0:T(512)S(1)} %fusion.54, f32[512]{0:T(512)S(1)} %get-tuple-element.147), kind=kOutput, calls=%fused_computation.6.clone.1 | convolution fusion | flops 171704320 | bytes 5968384 | tf_op jit(solution)/shard_map/while/body/eval_jaxpr/dot_general | solution.py:61
  115.2 2.9 %maximum_add_fusion.2 = f32[2560,128]{0,1:T(8,128)} fusion(f32[2560,64]{0,1:T(8,128)} %fusion.55, f32[2560,64]{0,1:T(8,128)} %fusion.56, f32[2560,128]{0,1:T(8,128)} %get-tuple-element.160, pred[]{:T(512)S(6)} %compare.3), kind=kLoop, calls=%fused_computation.8.clone.1 | loop fusion | flops 983040 | bytes 3932161 | tf_op jit(solution)/shard_map/while/body/eval_jaxpr/add | solution.py:62
  122.3 2.7 %multiply_reduce_fusion.2 = (f32[512]{0:T(512)S(1)}, f32[512,2560]{1,0:T(8,128)S(1)}) fusion(f32[512]{0:T(512)S(1)} %fusion.54, f32[512,2560]{1,0:T(8,128)S(1)} %get-tuple-element.146, f32[512]{0:T(512)S(1)} %get-tuple-element.147, bf16[2560,64]{1,0:T(8,128)(2,1)} %get-tuple-element.174, bf16[8,512,64]{1,2,0:T(8,128)(2,1)} %get-tuple-element.173, ...), kind=kOutput, calls=%fused_computation.1.clone.1 | convolution fusion | flops 173014528 | bytes 11213312 | tf_op jit(solution)/shard_map/while/body/eval_jaxpr/dot_general | solution.py:56
  129.0 2.8 %fusion.55 = f32[2560,64]{0,1:T(8,128)} fusion(bf16[8,512,64]{1,2,0:T(8,128)(2,1)} %get-tuple-element.173, s32[]{:T(128)} %get-tuple-element.159, f32[512,2560]{1,0:T(8,128)S(1)} %get-tuple-element.146, f32[512]{0:T(512)S(1)} %fusion.54, f32[512]{0:T(512)S(1)} %get-tuple-element.147), kind=kOutput, calls=%fused_computation.6.clone.1 | convolution fusion | flops 171704320 | bytes 5968384 | tf_op jit(solution)/shard_map/while/body/eval_jaxpr/dot_general | solution.py:61
  131.8 2.9 %maximum_add_fusion.2 = f32[2560,128]{0,1:T(8,128)} fusion(f32[2560,64]{0,1:T(8,128)} %fusion.55, f32[2560,64]{0,1:T(8,128)} %fusion.56, f32[2560,128]{0,1:T(8,128)} %get-tuple-element.160, pred[]{:T(512)S(6)} %compare.3), kind=kLoop, calls=%fused_computation.8.clone.1 | loop fusion | flops 983040 | bytes 3932161 | tf_op jit(solution)/shard_map/while/body/eval_jaxpr/add | solution.py:62
  138.9 2.7 %multiply_reduce_fusion.2 = (f32[512]{0:T(512)S(1)}, f32[512,2560]{1,0:T(8,128)S(1)}) fusion(f32[512]{0:T(512)S(1)} %fusion.54, f32[512,2560]{1,0:T(8,128)S(1)} %get-tuple-element.146, f32[512]{0:T(512)S(1)} %get-tuple-element.147, bf16[2560,64]{1,0:T(8,128)(2,1)} %get-tuple-element.174, bf16[8,512,64]{1,2,0:T(8,128)(2,1)} %get-tuple-element.173, ...), kind=kOutput, calls=%fused_computation.1.clone.1 | convolution fusion | flops 173014528 | bytes 11213312 | tf_op jit(solution)/shard_map/while/body/eval_jaxpr/dot_general | solution.py:56
  145.6 2.8 %fusion.55 = f32[2560,64]{0,1:T(8,128)} fusion(bf16[8,512,64]{1,2,0:T(8,128)(2,1)} %get-tuple-element.173, s32[]{:T(128)} %get-tuple-element.159, f32[512,2560]{1,0:T(8,128)S(1)} %get-tuple-element.146, f32[512]{0:T(512)S(1)} %fusion.54, f32[512]{0:T(512)S(1)} %get-tuple-element.147), kind=kOutput, calls=%fused_computation.6.clone.1 | convolution fusion | flops 171704320 | bytes 5968384 | tf_op jit(solution)/shard_map/while/body/eval_jaxpr/dot_general | solution.py:61
  148.4 2.9 %maximum_add_fusion.2 = f32[2560,128]{0,1:T(8,128)} fusion(f32[2560,64]{0,1:T(8,128)} %fusion.55, f32[2560,64]{0,1:T(8,128)} %fusion.56, f32[2560,128]{0,1:T(8,128)} %get-tuple-element.160, pred[]{:T(512)S(6)} %compare.3), kind=kLoop, calls=%fused_computation.8.clone.1 | loop fusion | flops 983040 | bytes 3932161 | tf_op jit(solution)/shard_map/while/body/eval_jaxpr/add | solution.py:62
  156.2 2.5 %collective-permute-start.4 = (bf16[512,128]{1,0:T(8,128)(2,1)S(1)}, bf16[512,128]{1,0:T(8,128)(2,1)S(1)}, u32[]{:S(2)}, u32[]{:S(2)}) collective-permute-start(bf16[512,128]{1,0:T(8,128)(2,1)S(1)} %get-tuple-element.96), channel_id=1, source_target_pairs={{0,24},{4,28},{8,0},{12,4},{16,8},{20,12},{24,16},{28,20},{1,25},{... | collective-permute-start | bytes 393224 | tf_op jit(solution)/shard_map/ppermute | solution.py:11
  158.7 3.5 %collective-permute-done.3 = bf16[512,128]{1,0:T(8,128)(2,1)S(1)} collective-permute-done((bf16[512,128]{1,0:T(8,128)(2,1)S(1)}, bf16[512,128]{1,0:T(8,128)(2,1)S(1)}, u32[]{:S(2)}, u32[]{:S(2)}) %collective-permute-start.3) | collective-permute-done | bytes 131104 | tf_op jit(solution)/shard_map/ppermute | solution.py:11
  164.9 7.0 %reduce-scatter.2.cloned.1.call-done = f32[256,128]{1,0:T(8,128)} async-done(((f32[512,128]{1,0:T(8,128)}), f32[256,128]{1,0:T(8,128)}) %reduce-scatter.2.cloned.1.call-update) | async-done | bytes 131088 | tf_op jit(solution)/shard_map/reduce_scatter | solution.py:68
  (67 shorter events, 72.7 us)
Async XLA Ops:
  7.2 164.8 %reduce-scatter.2.cloned.1.call-start = ((), (), s32[]{:S(2)}) async-start(), calls=%async_computation.1 | async-start | bytes 393216 | tf_op jit(solution)/shard_map/reduce_scatter | solution.py:68
  7.2 11.1 %collective-permute-start = (bf16[512,128]{1,0:T(8,128)(2,1)}, bf16[512,128]{1,0:T(8,128)(2,1)S(1)}, u32[]{:S(2)}, u32[]{:S(2)}) collective-permute-start(bf16[512,128]{1,0:T(8,128)(2,1)} %bitcast.70), channel_id=1, source_target_pairs={{0,24},{4,28},{8,0},{12,4},{16,8},{20,12},{24,16},{28,20},{1,25},{... | collective-permute-start | bytes 393224 | tf_op jit(solution)/shard_map/ppermute | solution.py:11
  12.3 7.0 %collective-permute-start.1 = (bf16[512,128]{1,0:T(8,128)(2,1)}, bf16[512,128]{1,0:T(8,128)(2,1)S(1)}, u32[]{:S(2)}, u32[]{:S(2)}) collective-permute-start(bf16[512,128]{1,0:T(8,128)(2,1)} %bitcast.71), channel_id=1, source_target_pairs={{0,8},{4,12},{8,16},{12,20},{16,24},{20,28},{24,0},{28,4},{1,9},{5... | collective-permute-start | bytes 393224 | tf_op jit(solution)/shard_map/ppermute | solution.py:11
  12.3 7.0 %collective-permute-start.2 = (bf16[512,128]{1,0:T(8,128)(2,1)}, bf16[512,128]{1,0:T(8,128)(2,1)S(1)}, u32[]{:S(2)}, u32[]{:S(2)}) collective-permute-start(bf16[512,128]{1,0:T(8,128)(2,1)} %bitcast.72), channel_id=1, source_target_pairs={{0,0},{2,2},{1,1},{3,3},{4,4},{6,6},{5,5},{7,7},{8,8},{10,10},{9,9... | collective-permute-start | bytes 393224 | tf_op jit(solution)/shard_map/ppermute | solution.py:11
  152.9 11.0 %copy-start = (bf16[8,512,64]{1,2,0:T(8,128)(2,1)S(1)}, bf16[8,512,64]{1,2,0:T(8,128)(2,1)}, u32[]{:S(2)}) copy-start(bf16[8,512,64]{1,2,0:T(8,128)(2,1)} %get-tuple-element.40) | copy-start | bytes 1572868
  154.8 7.4 %collective-permute-start.3 = (bf16[512,128]{1,0:T(8,128)(2,1)S(1)}, bf16[512,128]{1,0:T(8,128)(2,1)S(1)}, u32[]{:S(2)}, u32[]{:S(2)}) collective-permute-start(bf16[512,128]{1,0:T(8,128)(2,1)S(1)} %get-tuple-element.93), channel_id=1, source_target_pairs={{0,8},{4,12},{8,16},{12,20},{16,24},{20,28},{24,0},{28,4},{1,9},{5... | collective-permute-start | bytes 393224 | tf_op jit(solution)/shard_map/ppermute | solution.py:11
  156.2 6.9 %collective-permute-start.4 = (bf16[512,128]{1,0:T(8,128)(2,1)S(1)}, bf16[512,128]{1,0:T(8,128)(2,1)S(1)}, u32[]{:S(2)}, u32[]{:S(2)}) collective-permute-start(bf16[512,128]{1,0:T(8,128)(2,1)S(1)} %get-tuple-element.96), channel_id=1, source_target_pairs={{0,24},{4,28},{8,0},{12,4},{16,8},{20,12},{24,16},{28,20},{1,25},{... | collective-permute-start | bytes 393224 | tf_op jit(solution)/shard_map/ppermute | solution.py:11
  158.7 4.4 %collective-permute-start.5 = (bf16[512,128]{1,0:T(8,128)(2,1)S(1)}, bf16[512,128]{1,0:T(8,128)(2,1)S(1)}, u32[]{:S(2)}, u32[]{:S(2)}) collective-permute-start(bf16[512,128]{1,0:T(8,128)(2,1)S(1)} %get-tuple-element.95), channel_id=1, source_target_pairs={{0,0},{2,2},{1,1},{3,3},{4,4},{6,6},{5,5},{7,7},{8,8},{10,10},{9,9... | collective-permute-start | bytes 393224 | tf_op jit(solution)/shard_map/ppermute | solution.py:11
  158.7 4.4 %collective-permute-start.6 = (bf16[512,128]{1,0:T(8,128)(2,1)S(1)}, bf16[512,128]{1,0:T(8,128)(2,1)S(1)}, u32[]{:S(2)}, u32[]{:S(2)}) collective-permute-start(bf16[512,128]{1,0:T(8,128)(2,1)S(1)} %get-tuple-element.94), channel_id=1, source_target_pairs={{0,0},{2,2},{1,1},{3,3},{4,4},{6,6},{5,5},{7,7},{8,8},{10,10},{9,9... | collective-permute-start | bytes 393224 | tf_op jit(solution)/shard_map/ppermute | solution.py:11
Sparse Core Ops, SparseCore 0:
  164.0 7.8 reduce-scatter.1
where the time goes:
time: 181 us; the launch traced here: 179 us
  matrix products  88.8 us (49%)
  other arithmetic  44.4 us (25%)
  between operations  14.1 us (8%)
  waiting for transfers between devices  12.4 us (7%)
  starting transfers between devices  10 us (6%)
  local copies, waits for them, and re-layouts  9.02 us (5%)
    add x8, other arithmetic, one_head(): return (carry + jnp.concatenate([dkeys, dvalues], axis=1), dq_one)  23 us
    dot_general x8, matrix products, one_head(): dvalues = jnp.dot(probs_low.T, d_one, preferred_element_type=jnp.float32)  22.1 us
    dot_general x8, matrix products, one_head(): dprobs = jnp.dot(d_one, values.T, preferred_element_type=jnp.float32)  21.8 us
    dot_general x8, matrix products, one_head(): dkeys = jnp.dot(dscore.T, q_one, preferred_element_type=jnp.float32)  18.1 us
    dot_general x8, matrix products, one_head(): scores = jnp.dot(q_one, keys.T, preferred_element_type=jnp.float32) * scale  14.4 us
    convert_element_type x8, other arithmetic, one_head(): dscore = (probs * (dprobs - delta) * scale).astype(jnp.bfloat16)  13.8 us
    dot_general x8, matrix products, one_head(): jnp.dot(dscore, keys, preferred_element_type=jnp.float32)  12.4 us
    ppermute x7, starting transfers between devices, passed_along(): lax.ppermute(array, axis, [(i, (i + by) % peers) for i in range(peers)])  9.97 us
  transfers between devices with their start and end apart: 8, of which 4 were waited for; matrix products, arithmetic and copies ran while one was open for 3% of the time, Pallas kernels for 0%

commit v1 on v0

v1 whole, which is shorter than its diff:
```python
import functools

import jax
import jax.numpy as jnp
from jax import lax
from jax.experimental import pallas as pl
from jax.experimental.pallas import tpu as pltpu
from jax.sharding import PartitionSpec as P

HEAD_DIM = 64
REACH = 2
MESH = pl.DeviceIdType.MESH
F32 = jnp.float32
BF16 = jnp.bfloat16


def tile_groups(n_lat, n_lon):
    counts = {}
    for dlat, dlon in ((0, 0), (REACH, 0), (-REACH, 0), (0, REACH), (0, -REACH)):
        at = (dlat % n_lat, dlon % n_lon)
        counts[at] = counts.get(at, 0) + 1
    return list(counts.items())


def kernel(
    groups, sizes, q_ref, kv_ref, d_ref, dq_ref, dkv_ref,
    kvb, feats, rhs, so, sa, sb, pown, pa, pb, acc, dqt, keyt, kept, xs, xr, gs, gr, xos, xor_,
    kv_send, kv_recv, fw_send, fw_recv, xs_send, xs_recv, g_send, g_recv, o_send, o_recv,
):
    n_lat, n_lon, n_head = sizes
    tok = kv_ref.shape[0]
    dim = HEAD_DIM
    n_heads = q_ref.shape[1] // dim
    part = tok // n_head
    n_near = len(groups) - 1
    scale = 1.0 / dim**0.5
    lat, lon, head = (lax.axis_index(a) for a in ("lat", "lon", "head"))
    mine = pl.ds(pl.multiple_of(head * part, part), part)

    def at(off, sign):
        return {
            "lat": lax.rem(lat + (sign * off[0]) % n_lat, n_lat),
            "lon": lax.rem(lon + (sign * off[1]) % n_lon, n_lon),
            "head": head,
        }

    def fellow(step):
        return {"lat": lat, "lon": lon, "head": lax.rem(head + step, n_head)}

    def send(src, dst, s_sem, r_sem, to):
        copy = pltpu.make_async_remote_copy(
            src_ref=src, dst_ref=dst, send_sem=s_sem, recv_sem=r_sem, device_id=to, device_id_type=MESH
        )
        copy.start()
        return copy

    barrier = pltpu.get_barrier_semaphore()
    for off, _ in groups[1:]:
        pl.semaphore_signal(barrier, inc=1, device_id=at(off, -1), device_id_type=MESH)
    for step in range(1, n_head):
        pl.semaphore_signal(barrier, inc=1, device_id=fellow(step), device_id_type=MESH)
    pl.semaphore_wait(barrier, n_near + n_head - 1)

    kv_copies = [
        send(kv_ref.at[mine], kvb.at[b, mine], kv_send.at[b], kv_recv.at[b], at(off, -1))
        for b, (off, _) in enumerate(groups[1:])
    ]

    lane = lax.broadcasted_iota(jnp.int32, (tok, 2 * dim), 1)
    low = lane < dim

    def prepare(i, carry):
        cols = pl.ds(pl.multiple_of(i * 2 * dim, 2 * dim), 2 * dim)
        q_two = q_ref[:, cols].astype(F32) * scale
        d_two = d_ref[:, cols].astype(F32)
        q_swap = jnp.concatenate([q_two[:, dim:], q_two[:, :dim]], axis=1)
        d_swap = jnp.concatenate([d_two[:, dim:], d_two[:, :dim]], axis=1)
        for k, (q_one, d_one) in enumerate(((q_two, d_swap), (q_swap, d_two))):
            q_low = jnp.where(low, q_one, 0.0).astype(BF16)
            d_high = jnp.where(low, 0.0, d_one).astype(BF16)
            feats[2 * i + k, :tok] = q_low
            feats[2 * i + k, tok:] = d_high
            rhs[2 * i + k, :, :tok] = q_low.T
            rhs[2 * i + k, :, tok:] = d_high.T
        for k in range(2):
            so[2 * i + k] = jnp.dot(kv_ref[...], rhs[2 * i + k], preferred_element_type=F32)
        return carry

    half = n_heads // 4
    keyt[0] = kv_ref[...].T[:dim]
    lax.fori_loop(0, half, prepare, 0)
    fw_copies = []
    for b in range(n_near):
        kv_copies[b].wait()
        for step in range(1, n_head):
            fw_copies.append(
                send(kvb.at[b, mine], kvb.at[b, mine], fw_send.at[b, step], fw_recv.at[b, step], fellow(step))
            )
    lax.fori_loop(half, n_heads // 2, prepare, 0)
    for copy in fw_copies:
        copy.wait()
    for b in range(n_near):
        keyt[1 + b] = kvb[b].T[:dim]

    def scores(h, s_ref):
        for b in range(n_near):
            s_ref[b] = jnp.dot(kvb[b], rhs[h], preferred_element_type=F32)

    rows, width = 64, 256

    def weights(h, s_ref, p_ref):
        for t in range(0, tok, width):
            s_cols, d_cols = pl.ds(t, width), pl.ds(tok + t, width)
            chunks = [(0, r) for r in range(0, tok, rows)] + [
                (1 + b, r) for b in range(n_near) for r in range(0, tok, rows)
            ]

            def load(b, r, cols):
                if b == 0:
                    return so[h, pl.ds(r, rows), cols]
                return s_ref[b - 1, pl.ds(r, rows), cols]

            def fold(x):
                return x.reshape(rows // 8, 8, width)

            top = None
            for b, r in chunks:
                m = jnp.max(fold(load(b, r, s_cols)), axis=0)
                top = m if top is None else jnp.maximum(top, m)
            top = jnp.max(top, axis=0, keepdims=True)
            sums, dots = 0.0, 0.0
            for b, (_, times) in enumerate(groups):
                l, e_d = 0.0, 0.0
                for r in range(0, tok, rows):
                    e = jnp.exp(load(b, r, s_cols) - top)
                    if b == 0:
                        so[h, pl.ds(r, rows), s_cols] = e
                    else:
                        s_ref[b - 1, pl.ds(r, rows), s_cols] = e
                    l = l + jnp.sum(fold(e), axis=0)
                    e_d = e_d + jnp.sum(fold(e * load(b, r, d_cols)), axis=0)
                sums = sums + times * l
                dots = dots + times * e_d
            total = jnp.sum(sums, axis=0, keepdims=True)
            inv = 1.0 / total
            delta = jnp.sum(dots, axis=0, keepdims=True) / total
            for b, r in chunks:
                p = load(b, r, s_cols) * inv
                ds = (p * (load(b, r, d_cols) - delta)).astype(BF16)
                if b == 0:
                    pown[h, pl.ds(r, rows), s_cols] = ds
                    pown[h, pl.ds(r, rows), d_cols] = p.astype(BF16)
                else:
                    p_ref[b - 1, pl.ds(r, rows), s_cols] = ds
                    p_ref[b - 1, pl.ds(r, rows), d_cols] = p.astype(BF16)

    def grads(h, p_ref):
        dq = jnp.dot(keyt[0], pown[h, :, :tok], preferred_element_type=F32) * (groups[0][1] * scale)
        for b in range(n_near):
            dq += jnp.dot(keyt[1 + b], p_ref[b, :, :tok], preferred_element_type=F32) * (groups[1 + b][1] * scale)
            acc[b] += jnp.dot(p_ref[b], feats[h], preferred_element_type=F32)
        dqt[h] = dq.astype(BF16)

    acc[...] = jnp.zeros_like(acc)

    def pair(i, carry):
        scores(2 * i, sa)
        scores(2 * i + 1, sb)
        weights(2 * i, sa, pa)
        weights(2 * i + 1, sb, pb)
        grads(2 * i, pa)
        grads(2 * i + 1, pb)
        return carry

    lax.fori_loop(0, n_heads // 2, pair, 0)

    def rows_of(step):
        return pl.ds(pl.multiple_of(lax.rem(head + step, n_head) * part, part), part)

    x_copies = []
    for b in range(n_near):
        for step in range(1, n_head):
            xs[b, step] = (acc[b, rows_of(step)] * groups[1 + b][1]).astype(BF16)
            x_copies.append(send(xs.at[b, step], xr.at[b, step], xs_send.at[b, step], xs_recv.at[b, step], fellow(step)))

    def own(h, total):
        return total + jnp.dot(pown[h], feats[h], preferred_element_type=F32)

    def own_into(first, last):
        kept[...] = lax.fori_loop(first, last, own, kept[...])

    kept[...] = jnp.zeros_like(kept)
    own_into(0, n_heads // 4)
    g_copies = []
    for copy in x_copies:
        copy.wait()
    for b, (off, times) in enumerate(groups[1:]):
        total = acc[b, mine] * times
        for step in range(1, n_head):
            total += xr[b, step].astype(F32)
        gs[b] = total.astype(BF16)
        g_copies.append(send(gs.at[b], gr.at[b], g_send.at[b], g_recv.at[b], at(off, 1)))
    own_into(n_heads // 4, n_heads)
    o_copies = []
    for step in range(1, n_head):
        xos[step] = kept[rows_of(step)]
        o_copies.append(send(xos.at[step], xor_.at[step], o_send.at[step], o_recv.at[step], fellow(step)))
    for j in range(n_heads // 2):
        two = jnp.concatenate([dqt[2 * j], dqt[2 * j + 1]], axis=0)
        dq_ref[:, 2 * dim * j : 2 * dim * (j + 1)] = two.T
    for copy in o_copies:
        copy.wait()
    total = kept[mine]
    for step in range(1, n_head):
        total += xor_[step]
    total = total * groups[0][1]
    for b, copy in enumerate(g_copies):
        copy.wait()
        total += gr[b].astype(F32)
    dkv_ref[...] = total


def local(sizes, queries, key_value, dout):
    n_head = sizes[2]
    tok, width = key_value.shape[2:]
    n_heads = queries.shape[3] // HEAD_DIM
    groups = tile_groups(sizes[0], sizes[1])
    near = max(len(groups) - 1, 1)
    part = tok // n_head
    vmem = pl.BlockSpec(memory_space=pltpu.VMEM)
    dma = pltpu.SemaphoreType.DMA
    keys = len(groups) * tok
    dq, dkv = pl.pallas_call(
        functools.partial(kernel, groups, sizes),
        out_shape=(
            jax.ShapeDtypeStruct((tok, n_heads * HEAD_DIM), BF16),
            jax.ShapeDtypeStruct((part, width), F32),
        ),
        in_specs=[vmem] * 3,
        out_specs=(vmem, vmem),
        scratch_shapes=[
            pltpu.VMEM((near, tok, width), BF16),
            pltpu.VMEM((n_heads, 2 * tok, width), BF16),
            pltpu.VMEM((n_heads, width, 2 * tok), BF16),
            pltpu.VMEM((n_heads, tok, 2 * tok), F32),
            pltpu.VMEM((near, tok, 2 * tok), F32),
            pltpu.VMEM((near, tok, 2 * tok), F32),
            pltpu.VMEM((n_heads, tok, 2 * tok), BF16),
            pltpu.VMEM((near, tok, 2 * tok), BF16),
            pltpu.VMEM((near, tok, 2 * tok), BF16),
            pltpu.VMEM((near, tok, width), F32),
            pltpu.VMEM((n_heads, HEAD_DIM, tok), BF16),
            pltpu.VMEM((near + 1, HEAD_DIM, tok), BF16),
            pltpu.VMEM((tok, width), F32),
            pltpu.VMEM((near, n_head, part, width), BF16),
            pltpu.VMEM((near, n_head, part, width), BF16),
            pltpu.VMEM((near, part, width), BF16),
            pltpu.VMEM((near, part, width), BF16),
            pltpu.VMEM((n_head, part, width), F32),
            pltpu.VMEM((n_head, part, width), F32),
            dma((near,)), dma((near,)),
            dma((near, n_head)), dma((near, n_head)),
            dma((near, n_head)), dma((near, n_head)),
            dma((near,)), dma((near,)),
            dma((n_head,)), dma((n_head,)),
        ],
        compiler_params=pltpu.CompilerParams(
            collective_id=0, has_side_effects=True, vmem_limit_bytes=60 * 2**20
        ),
        cost_estimate=pl.CostEstimate(
            flops=10 * n_heads * tok * keys * HEAD_DIM,
            bytes_accessed=8 * tok * n_heads * HEAD_DIM,
            transcendentals=n_heads * tok * keys,
        ),
    )(queries[0, 0], key_value[0, 0], dout[0, 0])
    return dq[None, None], dkv[None, None]


def solution(mesh):
    sizes = tuple(mesh.shape[a] for a in ("lat", "lon", "head"))
    placed = P("lat", "lon", None, "head")
    return jax.shard_map(
        functools.partial(local, sizes),
        mesh=mesh,
        in_specs=(placed, P("lat", "lon", None, None), placed),
        out_specs=(placed, P("lat", "lon", "head", None)),
        check_vma=False,
    )
```

time: 181 us -> 44 us (0.24); the launches traced: 179 us -> 43.9 us
  matrix products: 88.8 us -> 0 us
  other arithmetic: 44.4 us -> 0 us
  Pallas kernels: 0 us -> 40.7 us
  between operations: 14.1 us -> 0.65 us
  waiting for transfers between devices: 12.4 us -> 0 us
  starting transfers between devices: 10 us -> 0 us
  local copies, waits for them, and re-layouts: 9.02 us -> 2.56 us
    dot_general x40 -> x0, matrix products: 88.8 us -> none  [the longest x8 22.1 us: one_head(): dvalues = jnp.dot(probs_low.T, d_one, preferred_element_type=jnp.float32)]
    pallas_call x0 -> x1, Pallas kernels: none -> 40.7 us  [local(): pl.pallas_call(functools.partial(kernel, groups, sizes), out_shape=(jax.S...]
    add x9 -> x0, other arithmetic: 23.8 us -> none  [the longest x8 23 us: one_head(): return (carry + jnp.concatenate([dkeys, dvalues], axis=1), dq_one)]
    convert_element_type x8 -> x0, other arithmetic: 13.8 us -> none  [one_head(): dscore = (probs * (dprobs - delta) * scale).astype(jnp.bfloat16)]
    ppermute x7 -> x0, starting transfers between devices: 9.97 us -> none  [passed_along(): lax.ppermute(array, axis, [(i, (i + by) % peers) for i in range(peers)])]
    reduce_scatter x1 -> x0, waiting for transfers between devices: 7.02 us -> none  [local(): lax.psum_scatter(send_back(parts), 'head', scatter_dimension=0, tiled=True)]
    reduce_sum x8 -> x0, other arithmetic: 6.75 us -> none  [one_head(): probs = expo / jnp.sum(expo, axis=-1, keepdims=True)]
    ppermute x7 -> x0, waiting for transfers between devices: 5.34 us -> none  [passed_along(): lax.ppermute(array, axis, [(i, (i + by) % peers) for i in range(peers)])]
  transfers between devices with their start and end apart: 8 -> 0, of which waited for: 4 -> 0; matrix products, arithmetic and copies ran while one was open for 3% -> 0% of each run, Pallas kernels for 0% -> 0%
where the time goes in v1:
time: 44 us; the launch traced here: 43.9 us
  Pallas kernels  40.7 us (93%)
  local copies, waits for them, and re-layouts  2.56 us (6%)
  between operations  0.65 us (1%)
    pallas_call x1, Pallas kernels, local(): pl.pallas_call(functools.partial(kernel, groups, sizes), out_shape=(jax.S...  40.7 us
    unnamed x4, local copies, waits for them, and re-layouts  2.56 us

profile of v1, /device:TPU:0, one launch (start us, length us, event | category | flops | bytes accessed | tf_op | source)
XLA Modules:
  0.0 43.9 jit_solution(16334275302492670796)
XLA Ops:
  0.6 40.7 %shard_map.50 = (bf16[512,512]{1,0:T(8,128)(2,1)}, f32[256,128]{1,0:T(8,128)}) custom-call(bf16[512,512]{1,0:T(8,128)(2,1)} %bitcast.7, bf16[512,128]{1,0:T(8,128)(2,1)} %bitcast.9, bf16[512,512]{1,0:T(8,128)(2,1)} %bitcast.8), custom_call_target="tpu_custom_call" | custom-call | flops 4026531840 | bytes 2097152 | tf_op jit(solution)/shard_map/pallas_call | solution.py:233
  41.3 0.0 copy-start
  41.3 1.9 %copy.7 = bf16[1,1,512,512]{3,2,1,0:T(8,128)(2,1)} copy(bf16[1,1,512,512]{3,2,1,0:T(8,128)(2,1)} %bitcast.5) | data formatting | bytes 1048576
  43.2 0.0 copy-done
  43.2 0.7 %copy.8 = f32[1,1,256,128]{3,2,1,0:T(8,128)} copy(f32[1,1,256,128]{3,2,1,0:T(8,128)S(1)} %bitcast.6) | data formatting | bytes 262144
Async XLA Ops:
  41.3 1.9 %copy-start = (f32[256,128]{1,0:T(8,128)S(1)}, f32[256,128]{1,0:T(8,128)}, u32[]{:S(2)}) copy-start(f32[256,128]{1,0:T(8,128)} %get-tuple-element.5) | copy-start | bytes 393220

commit v2 on v1

v2 whole, which is shorter than its diff:
```python
import functools

import jax
import jax.numpy as jnp
from jax import lax
from jax.experimental import pallas as pl
from jax.experimental.pallas import tpu as pltpu
from jax.sharding import PartitionSpec as P

HEAD_DIM = 64
REACH = 2
DEEP = 2
MESH = pl.DeviceIdType.MESH
F32 = jnp.float32
BF16 = jnp.bfloat16


def tile_groups(n_lat, n_lon):
    counts = {}
    for dlat, dlon in ((0, 0), (REACH, 0), (-REACH, 0), (0, REACH), (0, -REACH)):
        at = (dlat % n_lat, dlon % n_lon)
        counts[at] = counts.get(at, 0) + 1
    return list(counts.items())


def interleave(*lists):
    ranked = []
    for k, tasks in enumerate(lists):
        ranked += [((j + 0.5) / len(tasks), k, j) for j in range(len(tasks))]
    for _, k, j in sorted(ranked):
        lists[k][j]()


def kernel(
    groups, sizes, q_ref, kv_ref, d_ref, dq_ref, dkv_ref,
    kvb, rhs, feats, so, sa, sb, pown, pa, pb, fa, fb, mo, ma, mb, acc, dqn, invs, keyt, keyn, kept,
    xs, xr, gs, gr, xos, xor_,
    kv_send, kv_recv, fw_send, fw_recv, xs_send, xs_recv, g_send, g_recv, o_send, o_recv,
):
    n_lat, n_lon, n_head = sizes
    tok = kv_ref.shape[0]
    dim = HEAD_DIM
    n_heads = q_ref.shape[1] // dim
    part = tok // n_head
    n_near = len(groups) - 1
    scale = 1.0 / dim**0.5
    lat, lon, head = (lax.axis_index(a) for a in ("lat", "lon", "head"))
    mine = pl.ds(pl.multiple_of(head * part, part), part)

    def at(off, sign):
        return {
            "lat": lax.rem(lat + (sign * off[0]) % n_lat, n_lat),
            "lon": lax.rem(lon + (sign * off[1]) % n_lon, n_lon),
            "head": head,
        }

    def fellow(step):
        return {"lat": lat, "lon": lon, "head": lax.rem(head + step, n_head)}

    def send(src, dst, s_sem, r_sem, to):
        copy = pltpu.make_async_remote_copy(
            src_ref=src, dst_ref=dst, send_sem=s_sem, recv_sem=r_sem, device_id=to, device_id_type=MESH
        )
        copy.start()
        return copy

    barrier = pltpu.get_barrier_semaphore()
    for off, _ in groups[1:]:
        pl.semaphore_signal(barrier, inc=1, device_id=at(off, -1), device_id_type=MESH)
    for step in range(1, n_head):
        pl.semaphore_signal(barrier, inc=1, device_id=fellow(step), device_id_type=MESH)
    pl.semaphore_wait(barrier, n_near + n_head - 1)

    kv_copies = [
        send(kv_ref.at[mine], kvb.at[b, mine], kv_send.at[b], kv_recv.at[b], at(off, -1))
        for b, (off, _) in enumerate(groups[1:])
    ]

    def fold(x):
        return x.reshape(x.shape[0] // 8, 8, x.shape[1])

    above = jnp.zeros((dim, tok), BF16)

    def prepare(i, carry):
        cols = pl.ds(pl.multiple_of(i * 2 * dim, 2 * dim), 2 * dim)
        q_two = (q_ref[:, cols].astype(F32) * scale).astype(BF16).T
        d_two = d_ref[:, cols].T
        for k in range(2):
            h = 2 * i + k
            rhs[h, :dim, :tok] = q_two[k * dim : (k + 1) * dim]
            rhs[h, dim:, :tok] = above
            rhs[h, :dim, tok:] = above
            rhs[h, dim:, tok:] = d_two[k * dim : (k + 1) * dim]
        for k in range(2):
            h = 2 * i + k
            top = None
            for r in range(0, tok, piece):
                s = jnp.dot(kv_ref[pl.ds(r, piece)], rhs[h, :, :tok], preferred_element_type=F32)
                so[h, pl.ds(r, piece), :tok] = s
                m = jnp.max(fold(s), axis=0)
                top = m if top is None else jnp.maximum(top, m)
                so[h, pl.ds(r, piece), tok:] = jnp.dot(
                    kv_ref[pl.ds(r, piece)], rhs[h, :, tok:], preferred_element_type=F32
                )
            mo[h] = top
        return carry

    piece = tok // 2
    half = n_heads // 4
    keyt[...] = kv_ref[...].T[:dim]
    lax.fori_loop(0, half, prepare, 0)
    fw_copies = []
    for b in range(n_near):
        kv_copies[b].wait()
        for step in range(1, n_head):
            fw_copies.append(
                send(kvb.at[b, mine], kvb.at[b, mine], fw_send.at[b, step], fw_recv.at[b, step], fellow(step))
            )
    lax.fori_loop(half, n_heads // 2, prepare, 0)
    for copy in fw_copies:
        copy.wait()
    for b in range(n_near):
        keyn[:, pl.ds(b * tok, tok)] = (kvb[b].T[:dim].astype(F32) * groups[1 + b][1]).astype(BF16)

    def score_tasks(h, s_ref, m_ref):
        tasks = []
        for b in range(n_near):
            for r in range(0, tok, piece):

                def score(b=b, r=r):
                    s = jnp.dot(kvb[b, pl.ds(r, piece)], rhs[h, :, :tok], preferred_element_type=F32)
                    s_ref[pl.ds(b * tok + r, piece), :tok] = s
                    m = jnp.max(fold(s), axis=0)
                    m_ref[...] = m if b + r == 0 else jnp.maximum(m_ref[...], m)

                def gain(b=b, r=r):
                    s_ref[pl.ds(b * tok + r, piece), tok:] = jnp.dot(
                        kvb[b, pl.ds(r, piece)], rhs[h, :, tok:], preferred_element_type=F32
                    )

                tasks += [score, gain]
        return tasks

    rows, width = 64, tok // 2

    def weight_tasks(h, s_ref, m_ref, p_ref, f_ref):
        tasks = []
        tops = {}
        for t in range(0, tok, width):
            s_cols, d_cols = pl.ds(t, width), pl.ds(tok + t, width)
            state = {}

            def begin(t=t, state=state, s_cols=s_cols):
                state["top"] = jnp.max(jnp.maximum(mo[h, :, s_cols], m_ref[:, s_cols]), axis=0, keepdims=True)
                state["sums"], state["dots"] = 0.0, 0.0

            def first(b, r, state=state, s_cols=s_cols, d_cols=d_cols):
                if b == 0:
                    s, dp = so[h, pl.ds(r, rows), s_cols], so[h, pl.ds(r, rows), d_cols]
                else:
                    at_row = pl.ds((b - 1) * tok + r, rows)
                    s, dp = s_ref[at_row, s_cols], s_ref[at_row, d_cols]
                e = jnp.exp(s - state["top"])
                low = e.astype(BF16)
                if b == 0:
                    pown[h, pl.ds(r, rows), d_cols] = low
                else:
                    p_ref[at_row, d_cols] = low
                times = groups[b][1]
                if r == 0:
                    state["l"], state["e"] = 0.0, 0.0
                state["l"] += jnp.sum(fold(e), axis=0)
                state["e"] += jnp.sum(fold(e * dp), axis=0)
                if r + rows == tok:
                    state["sums"] += times * state["l"]
                    state["dots"] += times * state["e"]

            def middle(t=t, state=state, s_cols=s_cols, d_cols=d_cols):
                total = jnp.sum(state["sums"], axis=0, keepdims=True)
                state["delta"] = jnp.sum(state["dots"], axis=0, keepdims=True) / total
                inv = 1.0 / total
                invs[h, :, s_cols] = inv
                for base, cols in ((t, s_cols), (tok + t, d_cols)):
                    scaled = (rhs[h, :, cols].astype(F32) * inv).astype(BF16).T
                    f_ref[pl.ds(base, width)] = scaled
                    feats[h, pl.ds(base, width)] = scaled

            def second(b, r, state=state, s_cols=s_cols, d_cols=d_cols):
                if b == 0:
                    low, dp = pown[h, pl.ds(r, rows), d_cols], so[h, pl.ds(r, rows), d_cols]
                    pown[h, pl.ds(r, rows), s_cols] = low * (dp - state["delta"]).astype(BF16)
                else:
                    at_row = pl.ds((b - 1) * tok + r, rows)
                    low, dp = p_ref[at_row, d_cols], s_ref[at_row, d_cols]
                    p_ref[at_row, s_cols] = low * (dp - state["delta"]).astype(BF16)

            chunks = [(b, r) for b in range(n_near + 1) for r in range(0, tok, rows)]
            tasks.append(begin)
            tasks += [functools.partial(first, b, r) for b, r in chunks]
            tasks.append(middle)
            tasks += [functools.partial(second, b, r) for b, r in chunks]
        return tasks

    def grad_tasks(h, p_ref, f_ref):
        tasks = []
        for b in range(n_near):
            for r in range(0, tok, piece):

                def grad(b=b, r=r):
                    acc[b, pl.ds(r, piece)] += jnp.dot(
                        p_ref[pl.ds(b * tok + r, piece)], f_ref[...], preferred_element_type=F32
                    )

                tasks.append(grad)

        def to_queries():
            dqn[h] = jnp.dot(keyn[...], p_ref[:, :tok], preferred_element_type=F32)

        if n_near:
            tasks.append(to_queries)
        return tasks

    acc[...] = jnp.zeros_like(acc)
    if not n_near:
        dqn[...] = jnp.zeros_like(dqn)
        ma[...] = jnp.full_like(ma, -jnp.inf)
        mb[...] = jnp.full_like(mb, -jnp.inf)
    even, odd = (sa, ma, pa, fa), (sb, mb, pb, fb)

    if n_near > DEEP:

        def one(h, carry):
            for tasks in (score_tasks(h, sa, ma), weight_tasks(h, *even), grad_tasks(h, pa, fa)):
                interleave(tasks)
            return carry

        lax.fori_loop(0, n_heads, one, 0)
    else:
        interleave(score_tasks(0, sa, ma))
        interleave(weight_tasks(0, *even), score_tasks(1, sb, mb))

        def pair(i, carry):
            h = 2 * i + 1
            interleave(weight_tasks(h, *odd), grad_tasks(h - 1, pa, fa) + score_tasks(h + 1, sa, ma))
            interleave(weight_tasks(h + 1, *even), grad_tasks(h, pb, fb) + score_tasks(h + 2, sb, mb))
            return carry

        lax.fori_loop(0, n_heads // 2 - 1, pair, 0)
        last = n_heads - 1
        interleave(weight_tasks(last, *odd), grad_tasks(last - 1, pa, fa))
        interleave(grad_tasks(last, pb, fb))

    def rows_of(step):
        return pl.ds(pl.multiple_of(lax.rem(head + step, n_head) * part, part), part)

    x_copies = []
    for b in range(n_near):
        for step in range(1, n_head):
            xs[b, step] = (acc[b, rows_of(step)] * groups[1 + b][1]).astype(BF16)
            x_copies.append(send(xs.at[b, step], xr.at[b, step], xs_send.at[b, step], xs_recv.at[b, step], fellow(step)))

    def own_pair(i, carry):
        for r in range(0, tok, piece):
            kept[pl.ds(r, piece)] += jnp.dot(
                pown[2 * i, pl.ds(r, piece)], feats[2 * i], preferred_element_type=F32
            ) + jnp.dot(pown[2 * i + 1, pl.ds(r, piece)], feats[2 * i + 1], preferred_element_type=F32)
        both = []
        for h in (2 * i, 2 * i + 1):
            dq = jnp.dot(keyt[...], pown[h, :, :tok], preferred_element_type=F32) * groups[0][1] + dqn[h]
            both.append((dq * (invs[h] * scale)).astype(BF16))
        cols = pl.ds(pl.multiple_of(i * 2 * dim, 2 * dim), 2 * dim)
        dq_ref[:, cols] = jnp.concatenate(both, axis=0).T
        return carry

    kept[...] = jnp.zeros_like(kept)
    lax.fori_loop(0, n_heads // 8, own_pair, 0)
    g_copies = []
    for copy in x_copies:
        copy.wait()
    for b, (off, times) in enumerate(groups[1:]):
        total = acc[b, mine] * times
        for step in range(1, n_head):
            total += xr[b, step].astype(F32)
        gs[b] = total.astype(BF16)
        g_copies.append(send(gs.at[b], gr.at[b], g_send.at[b], g_recv.at[b], at(off, 1)))
    lax.fori_loop(n_heads // 8, n_heads // 2, own_pair, 0)
    o_copies = []
    for step in range(1, n_head):
        xos[step] = kept[rows_of(step)]
        o_copies.append(send(xos.at[step], xor_.at[step], o_send.at[step], o_recv.at[step], fellow(step)))
    for copy in o_copies:
        copy.wait()
    total = kept[mine]
    for step in range(1, n_head):
        total += xor_[step]
    total = total * groups[0][1]
    for b, copy in enumerate(g_copies):
        copy.wait()
        total += gr[b].astype(F32)
    dkv_ref[...] = total


def local(sizes, queries, key_value, dout):
    n_head = sizes[2]
    tok, width = key_value.shape[2:]
    n_heads = queries.shape[3] // HEAD_DIM
    groups = tile_groups(sizes[0], sizes[1])
    near = max(len(groups) - 1, 1)
    second = near * tok if near <= DEEP else 16
    part = tok // n_head
    vmem = pl.BlockSpec(memory_space=pltpu.VMEM)
    dma = pltpu.SemaphoreType.DMA
    keys = len(groups) * tok
    dq, dkv = pl.pallas_call(
        functools.partial(kernel, groups, sizes),
        out_shape=(
            jax.ShapeDtypeStruct((tok, n_heads * HEAD_DIM), BF16),
            jax.ShapeDtypeStruct((part, width), F32),
        ),
        in_specs=[vmem] * 3,
        out_specs=(vmem, vmem),
        scratch_shapes=[
            pltpu.VMEM((near, tok, width), BF16),
            pltpu.VMEM((n_heads, width, 2 * tok), BF16),
            pltpu.VMEM((n_heads, 2 * tok, width), BF16),
            pltpu.VMEM((n_heads, tok, 2 * tok), F32),
            pltpu.VMEM((near * tok, 2 * tok), F32),
            pltpu.VMEM((second, 2 * tok), F32),
            pltpu.VMEM((n_heads, tok, 2 * tok), BF16),
            pltpu.VMEM((near * tok, 2 * tok), BF16),
            pltpu.VMEM((second, 2 * tok), BF16),
            pltpu.VMEM((2 * tok, width), BF16),
            pltpu.VMEM((2 * tok, width), BF16),
            pltpu.VMEM((n_heads, 8, tok), F32),
            pltpu.VMEM((8, tok), F32),
            pltpu.VMEM((8, tok), F32),
            pltpu.VMEM((near, tok, width), F32),
            pltpu.VMEM((n_heads, HEAD_DIM, tok), F32),
            pltpu.VMEM((n_heads, 1, tok), F32),
            pltpu.VMEM((HEAD_DIM, tok), BF16),
            pltpu.VMEM((HEAD_DIM, near * tok), BF16),
            pltpu.VMEM((tok, width), F32),
            pltpu.VMEM((near, n_head, part, width), BF16),
            pltpu.VMEM((near, n_head, part, width), BF16),
            pltpu.VMEM((near, part, width), BF16),
            pltpu.VMEM((near, part, width), BF16),
            pltpu.VMEM((n_head, part, width), F32),
            pltpu.VMEM((n_head, part, width), F32),
            dma((near,)), dma((near,)),
            dma((near, n_head)), dma((near, n_head)),
            dma((near, n_head)), dma((near, n_head)),
            dma((near,)), dma((near,)),
            dma((n_head,)), dma((n_head,)),
        ],
        compiler_params=pltpu.CompilerParams(
            collective_id=0, has_side_effects=True, vmem_limit_bytes=62 * 2**20
        ),
        cost_estimate=pl.CostEstimate(
            flops=10 * n_heads * tok * keys * HEAD_DIM,
            bytes_accessed=8 * tok * n_heads * HEAD_DIM,
            transcendentals=n_heads * tok * keys,
        ),
    )(queries[0, 0], key_value[0, 0], dout[0, 0])
    return dq[None, None], dkv[None, None]


def solution(mesh):
    sizes = tuple(mesh.shape[a] for a in ("lat", "lon", "head"))
    placed = P("lat", "lon", None, "head")
    return jax.shard_map(
        functools.partial(local, sizes),
        mesh=mesh,
        in_specs=(placed, P("lat", "lon", None, None), placed),
        out_specs=(placed, P("lat", "lon", "head", None)),
        check_vma=False,
    )
```

time: 44 us -> 45 us (1.023)
  Pallas kernels: 40.7 us -> 41.6 us
    pallas_call x1, Pallas kernels: 40.7 us -> 41.6 us  [local(): pl.pallas_call(functools.partial(kernel, groups, sizes), out_shape=(jax.S...]
where the time goes in v2:
time: 45 us; the launch traced here: 44.8 us
  Pallas kernels  41.6 us (92%)
  local copies, waits for them, and re-layouts  2.56 us (6%)
  between operations  0.65 us (1%)
    pallas_call x1, Pallas kernels, local(): pl.pallas_call(functools.partial(kernel, groups, sizes), out_shape=(jax.S...  41.6 us
    unnamed x4, local copies, waits for them, and re-layouts  2.56 us

profile of v2, /device:TPU:0, one launch (start us, length us, event | category | flops | bytes accessed | tf_op | source)
XLA Modules:
  0.0 44.8 jit_solution(9396689980701823568)
XLA Ops:
  0.6 41.6 %shard_map.50 = (bf16[512,512]{1,0:T(8,128)(2,1)}, f32[256,128]{1,0:T(8,128)}) custom-call(bf16[512,512]{1,0:T(8,128)(2,1)} %bitcast.7, bf16[512,128]{1,0:T(8,128)(2,1)} %bitcast.9, bf16[512,512]{1,0:T(8,128)(2,1)} %bitcast.8), custom_call_target="tpu_custom_call" | custom-call | flops 4026531840 | bytes 2097152 | tf_op jit(solution)/shard_map/pallas_call | solution.py:314
  42.2 0.0 copy-start
  42.2 1.9 %copy.7 = bf16[1,1,512,512]{3,2,1,0:T(8,128)(2,1)} copy(bf16[1,1,512,512]{3,2,1,0:T(8,128)(2,1)} %bitcast.5) | data formatting | bytes 1048576
  44.1 0.0 copy-done
  44.1 0.7 %copy.8 = f32[1,1,256,128]{3,2,1,0:T(8,128)} copy(f32[1,1,256,128]{3,2,1,0:T(8,128)S(1)} %bitcast.6) | data formatting | bytes 262144
Async XLA Ops:
  42.2 1.9 %copy-start = (f32[256,128]{1,0:T(8,128)S(1)}, f32[256,128]{1,0:T(8,128)}, u32[]{:S(2)}) copy-start(f32[256,128]{1,0:T(8,128)} %get-tuple-element.5) | copy-start | bytes 393220

commit v3 on v2

--- a/solution.py
+++ b/solution.py
@@ -33,7 +33,7 @@
 
 def kernel(
     groups, sizes, q_ref, kv_ref, d_ref, dq_ref, dkv_ref,
-    kvb, rhs, feats, so, sa, sb, pown, pa, pb, fa, fb, mo, ma, mb, acc, dqn, invs, keyt, keyn, kept,
+    kvb, rhs, feats, so, sa, sb, pown, pa, pb, fa, fb, mo, ma, mb, acc, dqn, invs, delta, keyt, keyn, kept,
     xs, xr, gs, gr, xos, xor_,
     kv_send, kv_recv, fw_send, fw_recv, xs_send, xs_recv, g_send, g_recv, o_send, o_recv,
 ):
@@ -105,7 +105,7 @@
             mo[h] = top
         return carry
 
-    piece = tok // 2
+    piece = tok
     half = n_heads // 4
     keyt[...] = kv_ref[...].T[:dim]
     lax.fori_loop(0, half, prepare, 0)
@@ -143,14 +143,18 @@
 
     rows, width = 64, tok // 2
 
-    def weight_tasks(h, s_ref, m_ref, p_ref, f_ref):
+    def near_rows(b, r):
+        return pl.ds((b - 1) * tok + r, rows)
+
+    chunks = [(b, r) for b in range(n_near + 1) for r in range(0, tok, rows)]
+
+    def first_tasks(h, s_ref, m_ref, p_ref, f_ref):
         tasks = []
-        tops = {}
         for t in range(0, tok, width):
             s_cols, d_cols = pl.ds(t, width), pl.ds(tok + t, width)
             state = {}
 
-            def begin(t=t, state=state, s_cols=s_cols):
+            def begin(state=state, s_cols=s_cols):
                 state["top"] = jnp.max(jnp.maximum(mo[h, :, s_cols], m_ref[:, s_cols]), axis=0, keepdims=True)
                 state["sums"], state["dots"] = 0.0, 0.0
 
@@ -158,46 +162,54 @@
                 if b == 0:
                     s, dp = so[h, pl.ds(r, rows), s_cols], so[h, pl.ds(r, rows), d_cols]
                 else:
-                    at_row = pl.ds((b - 1) * tok + r, rows)
-                    s, dp = s_ref[at_row, s_cols], s_ref[at_row, d_cols]
+                    s, dp = s_ref[near_rows(b, r), s_cols], s_ref[near_rows(b, r), d_cols]
                 e = jnp.exp(s - state["top"])
-                low = e.astype(BF16)
                 if b == 0:
-                    pown[h, pl.ds(r, rows), d_cols] = low
+                    pown[h, pl.ds(r, rows), d_cols] = e.astype(BF16)
                 else:
-                    p_ref[at_row, d_cols] = low
-                times = groups[b][1]
+                    p_ref[near_rows(b, r), d_cols] = e.astype(BF16)
                 if r == 0:
                     state["l"], state["e"] = 0.0, 0.0
                 state["l"] += jnp.sum(fold(e), axis=0)
                 state["e"] += jnp.sum(fold(e * dp), axis=0)
                 if r + rows == tok:
-                    state["sums"] += times * state["l"]
-                    state["dots"] += times * state["e"]
-
-            def middle(t=t, state=state, s_cols=s_cols, d_cols=d_cols):
+                    state["sums"] += groups[b][1] * state["l"]
+                    state["dots"] += groups[b][1] * state["e"]
+
+            def finish(state=state, s_cols=s_cols):
                 total = jnp.sum(state["sums"], axis=0, keepdims=True)
-                state["delta"] = jnp.sum(state["dots"], axis=0, keepdims=True) / total
-                inv = 1.0 / total
-                invs[h, :, s_cols] = inv
+                delta[:, s_cols] = jnp.sum(state["dots"], axis=0, keepdims=True) / total
+                invs[h, :, s_cols] = 1.0 / total
+
+            tasks.append(begin)
+            tasks += [functools.partial(first, b, r) for b, r in chunks]
+            tasks.append(finish)
+        return tasks
+
+    def second_tasks(h, s_ref, m_ref, p_ref, f_ref):
+        tasks = []
+        for t in range(0, tok, width):
+            s_cols, d_cols = pl.ds(t, width), pl.ds(tok + t, width)
+
+            def features(t=t, s_cols=s_cols, d_cols=d_cols):
+                inv = invs[h, :, s_cols]
                 for base, cols in ((t, s_cols), (tok + t, d_cols)):
                     scaled = (rhs[h, :, cols].astype(F32) * inv).astype(BF16).T
                     f_ref[pl.ds(base, width)] = scaled
                     feats[h, pl.ds(base, width)] = scaled
 
-            def second(b, r, state=state, s_cols=s_cols, d_cols=d_cols):
+            def second(b, r, s_cols=s_cols, d_cols=d_cols):
                 if b == 0:
                     low, dp = pown[h, pl.ds(r, rows), d_cols], so[h, pl.ds(r, rows), d_cols]
-                    pown[h, pl.ds(r, rows), s_cols] = low * (dp - state["delta"]).astype(BF16)
                 else:
-                    at_row = pl.ds((b - 1) * tok + r, rows)
-                    low, dp = p_ref[at_row, d_cols], s_ref[at_row, d_cols]
-                    p_ref[at_row, s_cols] = low * (dp - state["delta"]).astype(BF16)
-
-            chunks = [(b, r) for b in range(n_near + 1) for r in range(0, tok, rows)]
-            tasks.append(begin)
-            tasks += [functools.partial(first, b, r) for b, r in chunks]
-            tasks.append(middle)
+                    low, dp = p_ref[near_rows(b, r), d_cols], s_ref[near_rows(b, r), d_cols]
+                ds = (low.astype(F32) * (dp - delta[:, s_cols])).astype(BF16)
+                if b == 0:
+                    pown[h, pl.ds(r, rows), s_cols] = ds
+                else:
+                    p_ref[near_rows(b, r), s_cols] = ds
+
+            tasks.append(features)
             tasks += [functools.partial(second, b, r) for b, r in chunks]
         return tasks
 
@@ -227,28 +239,39 @@
         mb[...] = jnp.full_like(mb, -jnp.inf)
     even, odd = (sa, ma, pa, fa), (sb, mb, pb, fb)
 
+    def block(*lists):
+        @pl.when(lat >= 0)
+        def _():
+            interleave(*lists)
+
     if n_near > DEEP:
 
         def one(h, carry):
-            for tasks in (score_tasks(h, sa, ma), weight_tasks(h, *even), grad_tasks(h, pa, fa)):
-                interleave(tasks)
+            block(score_tasks(h, sa, ma))
+            block(first_tasks(h, *even))
+            block(second_tasks(h, *even))
+            block(grad_tasks(h, pa, fa))
             return carry
 
         lax.fori_loop(0, n_heads, one, 0)
     else:
-        interleave(score_tasks(0, sa, ma))
-        interleave(weight_tasks(0, *even), score_tasks(1, sb, mb))
+        block(score_tasks(0, sa, ma))
+        block(first_tasks(0, *even), score_tasks(1, sb, mb))
+        block(second_tasks(0, *even))
 
         def pair(i, carry):
             h = 2 * i + 1
-            interleave(weight_tasks(h, *odd), grad_tasks(h - 1, pa, fa) + score_tasks(h + 1, sa, ma))
-            interleave(weight_tasks(h + 1, *even), grad_tasks(h, pb, fb) + score_tasks(h + 2, sb, mb))
+            block(first_tasks(h, *odd), score_tasks(h + 1, sa, ma))
+            block(second_tasks(h, *odd), grad_tasks(h - 1, pa, fa))
+            block(first_tasks(h + 1, *even), score_tasks(h + 2, sb, mb))
+            block(second_tasks(h + 1, *even), grad_tasks(h, pb, fb))
             return carry
 
         lax.fori_loop(0, n_heads // 2 - 1, pair, 0)
         last = n_heads - 1
-        interleave(weight_tasks(last, *odd), grad_tasks(last - 1, pa, fa))
-        interleave(grad_tasks(last, pb, fb))
+        block(first_tasks(last, *odd))
+        block(second_tasks(last, *odd), grad_tasks(last - 1, pa, fa))
+        block(grad_tasks(last, pb, fb))
 
     def rows_of(step):
         return pl.ds(pl.multiple_of(lax.rem(head + step, n_head) * part, part), part)
@@ -267,7 +290,7 @@
         both = []
         for h in (2 * i, 2 * i + 1):
             dq = jnp.dot(keyt[...], pown[h, :, :tok], preferred_element_type=F32) * groups[0][1] + dqn[h]
-            both.append((dq * (invs[h] * scale)).astype(BF16))
+            both.append(dq * (invs[h] * scale))
         cols = pl.ds(pl.multiple_of(i * 2 * dim, 2 * dim), 2 * dim)
         dq_ref[:, cols] = jnp.concatenate(both, axis=0).T
         return carry
@@ -293,11 +316,12 @@
     total = kept[mine]
     for step in range(1, n_head):
         total += xor_[step]
-    total = total * groups[0][1]
+    dkv_ref[0] = total * groups[0][1]
+    total = jnp.zeros_like(total)
     for b, copy in enumerate(g_copies):
         copy.wait()
         total += gr[b].astype(F32)
-    dkv_ref[...] = total
+    dkv_ref[1] = total
 
 
 def local(sizes, queries, key_value, dout):
@@ -314,8 +338,8 @@
     dq, dkv = pl.pallas_call(
         functools.partial(kernel, groups, sizes),
         out_shape=(
-            jax.ShapeDtypeStruct((tok, n_heads * HEAD_DIM), BF16),
-            jax.ShapeDtypeStruct((part, width), F32),
+            jax.ShapeDtypeStruct((tok, n_heads * HEAD_DIM), F32),
+            jax.ShapeDtypeStruct((2, part, width), F32),
         ),
         in_specs=[vmem] * 3,
         out_specs=(vmem, vmem),
@@ -337,6 +361,7 @@
             pltpu.VMEM((near, tok, width), F32),
             pltpu.VMEM((n_heads, HEAD_DIM, tok), F32),
             pltpu.VMEM((n_heads, 1, tok), F32),
+            pltpu.VMEM((1, tok), F32),
             pltpu.VMEM((HEAD_DIM, tok), BF16),
             pltpu.VMEM((HEAD_DIM, near * tok), BF16),
             pltpu.VMEM((tok, width), F32),
@@ -361,7 +386,7 @@
             transcendentals=n_heads * tok * keys,
         ),
     )(queries[0, 0], key_value[0, 0], dout[0, 0])
-    return dq[None, None], dkv[None, None]
+    return dq.astype(BF16)[None, None], (dkv[0] + dkv[1])[None, None]
 
 
 def solution(mesh):

time: 45 us -> 43.9 us (0.976)
  other arithmetic: 0 us -> 2.8 us
  local copies, waits for them, and re-layouts: 2.56 us -> 0.01 us
  Pallas kernels: 41.6 us -> 40.3 us
    unnamed x4 -> x2, local copies, waits for them, and re-layouts: 2.56 us -> 0.01 us
    broadcast_in_dim x0 -> x1, other arithmetic: none -> 2.13 us  [local(): return (dq.astype(BF16)[None, None], (dkv[0] + dkv[1])[None, None])]
    pallas_call x1, Pallas kernels: 41.6 us -> 40.3 us  [local(): pl.pallas_call(functools.partial(kernel, groups, sizes), out_shape=(jax.S...]
    add x0 -> x1, other arithmetic: none -> 0.67 us  [local(): return (dq.astype(BF16)[None, None], (dkv[0] + dkv[1])[None, None])]
where the time goes in v3:
time: 43.9 us; the launch traced here: 43.7 us
  Pallas kernels  40.3 us (92%)
  other arithmetic  2.8 us (6%)
  between operations  0.65 us (1%)
    pallas_call x1, Pallas kernels, local(): pl.pallas_call(functools.partial(kernel, groups, sizes), out_shape=(jax.S...  40.3 us
    broadcast_in_dim x1, other arithmetic, local(): return (dq.astype(BF16)[None, None], (dkv[0] + dkv[1])[None, None])  2.13 us

profile of v3, /device:TPU:0, one launch (start us, length us, event | category | flops | bytes accessed | tf_op | source)
XLA Modules:
  0.0 43.7 jit_solution(15002961946423944235)
XLA Ops:
  0.6 40.3 %shard_map.50 = (f32[512,512]{1,0:T(8,128)}, f32[2,256,128]{2,1,0:T(8,128)}) custom-call(bf16[512,512]{1,0:T(8,128)(2,1)} %bitcast.7, bf16[512,128]{1,0:T(8,128)(2,1)} %bitcast.9, bf16[512,512]{1,0:T(8,128)(2,1)} %bitcast.8), custom_call_target="tpu_custom_call" | custom-call | flops 4026531840 | bytes 2097152 | tf_op jit(solution)/shard_map/pallas_call | solution.py:338
  40.9 0.0 copy-start
  40.9 2.1 %convert_bitcast_fusion = bf16[1,1,512,512]{3,2,1,0:T(8,128)(2,1)} fusion(f32[512,512]{1,0:T(8,128)} %get-tuple-element.4), kind=kLoop, calls=%fused_computation | loop fusion | flops 262144 | bytes 1572864 | tf_op jit(solution)/shard_map/broadcast_in_dim | solution.py:389
  43.0 0.0 copy-done
  43.0 0.7 %add_bitcast_fusion = f32[1,1,256,128]{3,2,1,0:T(8,128)} fusion(f32[2,256,128]{2,1,0:T(8,128)S(1)} %copy-done), kind=kLoop, calls=%fused_computation.1 | loop fusion | flops 32768 | bytes 393216 | tf_op jit(solution)/shard_map/add | solution.py:389
Async XLA Ops:
  40.9 2.1 %copy-start = (f32[2,256,128]{2,1,0:T(8,128)S(1)}, f32[2,256,128]{2,1,0:T(8,128)}, u32[]{:S(2)}) copy-start(f32[2,256,128]{2,1,0:T(8,128)} %get-tuple-element.5) | copy-start | bytes 786436

commit v4 on v3

--- a/solution.py
+++ b/solution.py
@@ -69,13 +69,6 @@
         pl.semaphore_signal(barrier, inc=1, device_id=at(off, -1), device_id_type=MESH)
     for step in range(1, n_head):
         pl.semaphore_signal(barrier, inc=1, device_id=fellow(step), device_id_type=MESH)
-    pl.semaphore_wait(barrier, n_near + n_head - 1)
-
-    kv_copies = [
-        send(kv_ref.at[mine], kvb.at[b, mine], kv_send.at[b], kv_recv.at[b], at(off, -1))
-        for b, (off, _) in enumerate(groups[1:])
-    ]
-
     def fold(x):
         return x.reshape(x.shape[0] // 8, 8, x.shape[1])
 
@@ -106,9 +99,15 @@
         return carry
 
     piece = tok
-    half = n_heads // 4
+    half = 3 * n_heads // 8
     keyt[...] = kv_ref[...].T[:dim]
-    lax.fori_loop(0, half, prepare, 0)
+    prepare(0, 0)
+    pl.semaphore_wait(barrier, n_near + n_head - 1)
+    kv_copies = [
+        send(kv_ref.at[mine], kvb.at[b, mine], kv_send.at[b], kv_recv.at[b], at(off, -1))
+        for b, (off, _) in enumerate(groups[1:])
+    ]
+    lax.fori_loop(1, half, prepare, 0)
     fw_copies = []
     for b in range(n_near):
         kv_copies[b].wait()
@@ -287,10 +286,13 @@
             kept[pl.ds(r, piece)] += jnp.dot(
                 pown[2 * i, pl.ds(r, piece)], feats[2 * i], preferred_element_type=F32
             ) + jnp.dot(pown[2 * i + 1, pl.ds(r, piece)], feats[2 * i + 1], preferred_element_type=F32)
+        return carry
+
+    def own_queries(i, carry):
         both = []
         for h in (2 * i, 2 * i + 1):
             dq = jnp.dot(keyt[...], pown[h, :, :tok], preferred_element_type=F32) * groups[0][1] + dqn[h]
-            both.append(dq * (invs[h] * scale))
+            both.append((dq * invs[h]).astype(BF16))
         cols = pl.ds(pl.multiple_of(i * 2 * dim, 2 * dim), 2 * dim)
         dq_ref[:, cols] = jnp.concatenate(both, axis=0).T
         return carry
@@ -311,6 +313,7 @@
     for step in range(1, n_head):
         xos[step] = kept[rows_of(step)]
         o_copies.append(send(xos.at[step], xor_.at[step], o_send.at[step], o_recv.at[step], fellow(step)))
+    lax.fori_loop(0, n_heads // 2, own_queries, 0)
     for copy in o_copies:
         copy.wait()
     total = kept[mine]
@@ -338,7 +341,7 @@
     dq, dkv = pl.pallas_call(
         functools.partial(kernel, groups, sizes),
         out_shape=(
-            jax.ShapeDtypeStruct((tok, n_heads * HEAD_DIM), F32),
+            jax.ShapeDtypeStruct((tok, n_heads * HEAD_DIM), BF16),
             jax.ShapeDtypeStruct((2, part, width), F32),
         ),
         in_specs=[vmem] * 3,
@@ -386,7 +389,7 @@
             transcendentals=n_heads * tok * keys,
         ),
     )(queries[0, 0], key_value[0, 0], dout[0, 0])
-    return dq.astype(BF16)[None, None], (dkv[0] + dkv[1])[None, None]
+    return (dq * jnp.asarray(1.0 / HEAD_DIM**0.5, BF16))[None, None], (dkv[0] + dkv[1])[None, None]
 
 
 def solution(mesh):

time: 43.9 us -> 43.1 us (0.982)
  Pallas kernels: 40.3 us -> 39.7 us
    pallas_call x1, Pallas kernels: 40.3 us -> 39.7 us  [local(): pl.pallas_call(functools.partial(kernel, groups, sizes), out_shape=(jax.S...]
where the time goes in v4:
time: 43.1 us; the launch traced here: 42.9 us
  Pallas kernels  39.7 us (92%)
  other arithmetic  2.59 us (6%)
  between operations  0.65 us (2%)
    pallas_call x1, Pallas kernels, local(): pl.pallas_call(functools.partial(kernel, groups, sizes), out_shape=(jax.S...  39.7 us
    broadcast_in_dim x1, other arithmetic, local(): (dq * jnp.asarray(1.0 / HEAD_DIM ** 0.5, BF16))[None, None]  1.92 us

profile of v4, /device:TPU:0, one launch (start us, length us, event | category | flops | bytes accessed | tf_op | source)
XLA Modules:
  0.0 42.9 jit_solution(12956597706143545718)
XLA Ops:
  0.6 39.7 %shard_map.50 = (bf16[512,512]{1,0:T(8,128)(2,1)}, f32[2,256,128]{2,1,0:T(8,128)}) custom-call(bf16[512,512]{1,0:T(8,128)(2,1)} %bitcast.7, bf16[512,128]{1,0:T(8,128)(2,1)} %bitcast.9, bf16[512,512]{1,0:T(8,128)(2,1)} %bitcast.8), custom_call_target="tpu_custom_call" | custom-call | flops 4026531840 | bytes 2097152 | tf_op jit(solution)/shard_map/pallas_call | solution.py:341
  40.3 0.0 copy-start
  40.3 1.9 %multiply_bitcast_fusion = bf16[1,1,512,512]{3,2,1,0:T(8,128)(2,1)} fusion(bf16[512,512]{1,0:T(8,128)(2,1)} %get-tuple-element.4), kind=kLoop, calls=%fused_computation | loop fusion | flops 262144 | bytes 1048576 | tf_op jit(solution)/shard_map/broadcast_in_dim | solution.py:392
  42.2 0.0 copy-done
  42.2 0.7 %add_bitcast_fusion = f32[1,1,256,128]{3,2,1,0:T(8,128)} fusion(f32[2,256,128]{2,1,0:T(8,128)S(1)} %copy-done), kind=kLoop, calls=%fused_computation.1 | loop fusion | flops 32768 | bytes 393216 | tf_op jit(solution)/shard_map/add | solution.py:392
Async XLA Ops:
  40.3 1.9 %copy-start = (f32[2,256,128]{2,1,0:T(8,128)S(1)}, f32[2,256,128]{2,1,0:T(8,128)}, u32[]{:S(2)}) copy-start(f32[2,256,128]{2,1,0:T(8,128)} %get-tuple-element.5) | copy-start | bytes 786436

commit v5 on v4

--- a/solution.py
+++ b/solution.py
@@ -33,7 +33,7 @@
 
 def kernel(
     groups, sizes, q_ref, kv_ref, d_ref, dq_ref, dkv_ref,
-    kvb, rhs, feats, so, sa, sb, pown, pa, pb, fa, fb, mo, ma, mb, acc, dqn, invs, delta, keyt, keyn, kept,
+    kvb, rhs, feats, so, sa, sb, pown, pa, pb, fa, fb, mo, ma, mb, flat, acc, dqn, invs, delta, keyt, keyn, kept,
     xs, xr, gs, gr, xos, xor_,
     kv_send, kv_recv, fw_send, fw_recv, xs_send, xs_recv, g_send, g_recv, o_send, o_recv,
 ):
@@ -71,6 +71,9 @@
         pl.semaphore_signal(barrier, inc=1, device_id=fellow(step), device_id_type=MESH)
     def fold(x):
         return x.reshape(x.shape[0] // 8, 8, x.shape[1])
+
+    def across(a, b):
+        return lax.dot_general(a, b, (((1,), (1,)), ((), ())), preferred_element_type=F32)
 
     above = jnp.zeros((dim, tok), BF16)
 
@@ -193,9 +196,9 @@
             def features(t=t, s_cols=s_cols, d_cols=d_cols):
                 inv = invs[h, :, s_cols]
                 for base, cols in ((t, s_cols), (tok + t, d_cols)):
-                    scaled = (rhs[h, :, cols].astype(F32) * inv).astype(BF16).T
-                    f_ref[pl.ds(base, width)] = scaled
-                    feats[h, pl.ds(base, width)] = scaled
+                    scaled = (rhs[h, :, cols].astype(F32) * inv).astype(BF16)
+                    f_ref[:, pl.ds(base, width)] = scaled
+                    feats[h, :, pl.ds(base, width)] = scaled
 
             def second(b, r, s_cols=s_cols, d_cols=d_cols):
                 if b == 0:
@@ -218,9 +221,7 @@
             for r in range(0, tok, piece):
 
                 def grad(b=b, r=r):
-                    acc[b, pl.ds(r, piece)] += jnp.dot(
-                        p_ref[pl.ds(b * tok + r, piece)], f_ref[...], preferred_element_type=F32
-                    )
+                    flat[b, :, pl.ds(r, piece)] += across(f_ref[...], p_ref[pl.ds(b * tok + r, piece)])
 
                 tasks.append(grad)
 
@@ -231,7 +232,7 @@
             tasks.append(to_queries)
         return tasks
 
-    acc[...] = jnp.zeros_like(acc)
+    flat[...] = jnp.zeros_like(flat)
     if not n_near:
         dqn[...] = jnp.zeros_like(dqn)
         ma[...] = jnp.full_like(ma, -jnp.inf)
@@ -272,6 +273,9 @@
         block(second_tasks(last, *odd), grad_tasks(last - 1, pa, fa))
         block(grad_tasks(last, pb, fb))
 
+    for b in range(n_near):
+        acc[b] = flat[b].T
+
     def rows_of(step):
         return pl.ds(pl.multiple_of(lax.rem(head + step, n_head) * part, part), part)
 
@@ -282,10 +286,8 @@
             x_copies.append(send(xs.at[b, step], xr.at[b, step], xs_send.at[b, step], xs_recv.at[b, step], fellow(step)))
 
     def own_pair(i, carry):
-        for r in range(0, tok, piece):
-            kept[pl.ds(r, piece)] += jnp.dot(
-                pown[2 * i, pl.ds(r, piece)], feats[2 * i], preferred_element_type=F32
-            ) + jnp.dot(pown[2 * i + 1, pl.ds(r, piece)], feats[2 * i + 1], preferred_element_type=F32)
+        for h in (2 * i, 2 * i + 1):
+            flat[0] += across(feats[h], pown[h])
         return carry
 
     def own_queries(i, carry):
@@ -297,7 +299,7 @@
         dq_ref[:, cols] = jnp.concatenate(both, axis=0).T
         return carry
 
-    kept[...] = jnp.zeros_like(kept)
+    flat[0] = jnp.zeros_like(flat[0])
     lax.fori_loop(0, n_heads // 8, own_pair, 0)
     g_copies = []
     for copy in x_copies:
@@ -309,6 +311,7 @@
         gs[b] = total.astype(BF16)
         g_copies.append(send(gs.at[b], gr.at[b], g_send.at[b], g_recv.at[b], at(off, 1)))
     lax.fori_loop(n_heads // 8, n_heads // 2, own_pair, 0)
+    kept[...] = flat[0].T
     o_copies = []
     for step in range(1, n_head):
         xos[step] = kept[rows_of(step)]
@@ -349,18 +352,19 @@
         scratch_shapes=[
             pltpu.VMEM((near, tok, width), BF16),
             pltpu.VMEM((n_heads, width, 2 * tok), BF16),
-            pltpu.VMEM((n_heads, 2 * tok, width), BF16),
+            pltpu.VMEM((n_heads, width, 2 * tok), BF16),
             pltpu.VMEM((n_heads, tok, 2 * tok), F32),
             pltpu.VMEM((near * tok, 2 * tok), F32),
             pltpu.VMEM((second, 2 * tok), F32),
             pltpu.VMEM((n_heads, tok, 2 * tok), BF16),
             pltpu.VMEM((near * tok, 2 * tok), BF16),
             pltpu.VMEM((second, 2 * tok), BF16),
-            pltpu.VMEM((2 * tok, width), BF16),
-            pltpu.VMEM((2 * tok, width), BF16),
+            pltpu.VMEM((width, 2 * tok), BF16),
+            pltpu.VMEM((width, 2 * tok), BF16),
             pltpu.VMEM((n_heads, 8, tok), F32),
             pltpu.VMEM((8, tok), F32),
             pltpu.VMEM((8, tok), F32),
+            pltpu.VMEM((near, width, tok), F32),
             pltpu.VMEM((near, tok, width), F32),
             pltpu.VMEM((n_heads, HEAD_DIM, tok), F32),
             pltpu.VMEM((n_heads, 1, tok), F32),

time: 43.1 us -> 43.5 us (level)
  no operation moved by 1% of the time
where the time goes in v5:
time: 43.5 us; the launch traced here: 43.3 us
  Pallas kernels  40.1 us (92%)
  other arithmetic  2.59 us (6%)
  between operations  0.65 us (1%)
    pallas_call x1, Pallas kernels, local(): pl.pallas_call(functools.partial(kernel, groups, sizes), out_shape=(jax.S...  40.1 us
    broadcast_in_dim x1, other arithmetic, local(): (dq * jnp.asarray(1.0 / HEAD_DIM ** 0.5, BF16))[None, None]  1.92 us

profile of v5, /device:TPU:0, one launch (start us, length us, event | category | flops | bytes accessed | tf_op | source)
XLA Modules:
  0.0 43.3 jit_solution(2224124211024910274)
XLA Ops:
  0.6 40.1 %shard_map.50 = (bf16[512,512]{1,0:T(8,128)(2,1)}, f32[2,256,128]{2,1,0:T(8,128)}) custom-call(bf16[512,512]{1,0:T(8,128)(2,1)} %bitcast.7, bf16[512,128]{1,0:T(8,128)(2,1)} %bitcast.9, bf16[512,512]{1,0:T(8,128)(2,1)} %bitcast.8), custom_call_target="tpu_custom_call" | custom-call | flops 4026531840 | bytes 2097152 | tf_op jit(solution)/shard_map/pallas_call | solution.py:344
  40.7 0.0 copy-start
  40.7 1.9 %multiply_bitcast_fusion = bf16[1,1,512,512]{3,2,1,0:T(8,128)(2,1)} fusion(bf16[512,512]{1,0:T(8,128)(2,1)} %get-tuple-element.4), kind=kLoop, calls=%fused_computation | loop fusion | flops 262144 | bytes 1048576 | tf_op jit(solution)/shard_map/broadcast_in_dim | solution.py:396
  42.6 0.0 copy-done
  42.6 0.7 %add_bitcast_fusion = f32[1,1,256,128]{3,2,1,0:T(8,128)} fusion(f32[2,256,128]{2,1,0:T(8,128)S(1)} %copy-done), kind=kLoop, calls=%fused_computation.1 | loop fusion | flops 32768 | bytes 393216 | tf_op jit(solution)/shard_map/add | solution.py:396
Async XLA Ops:
  40.7 1.9 %copy-start = (f32[2,256,128]{2,1,0:T(8,128)S(1)}, f32[2,256,128]{2,1,0:T(8,128)}, u32[]{:S(2)}) copy-start(f32[2,256,128]{2,1,0:T(8,128)} %get-tuple-element.5) | copy-start | bytes 786436
